TPU v7x, 512 devices: a whole 4x8x8 slice. The times are simulated.
512 devices in a mesh: tm: 16 (over z, core), space: 32 (over x, y).
Axes of the slice: x: 4, y: 8, z: 8, core: 2. Of those that a mesh axis runs over, the one named last changes fastest.
Arguments:
- queries: bfloat16 [16, 4096, 1120], P('tm', 'space'), may hold values from -6 to 6
- keys_in: bfloat16 [16, 4096, 1120], P('tm', 'space'), may hold values from -30 to 30
- values_in: bfloat16 [16, 4096, 1120], P('tm', 'space'), may hold values from -10 to 10
- grad_attn: bfloat16 [16, 4096, 1120], P('tm', 'space'), may hold values from -6 to 6
Outputs:
- mixed: bfloat16 [16, 4096, 1120], P('tm', 'space')
- grad_queries: bfloat16 [16, 4096, 1120], P('tm', 'space')
- grad_keys: bfloat16 [16, 4096, 1120], P('tm', 'space')
- values_gradient: bfloat16 [16, 4096, 1120], P('tm', 'space')
All inputs are finite; a program needn't handle non-finite values.
Results may differ from a plain program's by a relative error of at most 0.001.
Values sent between devices are 32-bit elements; how exact they have to be, the bound alone decides.
No kernel may reach another device: no remote copies, remote signals or barrier semaphores. Data moves between devices by JAX's collectives and lax.ppermute only.
A program may use at most 64 MiB of HBM per device.

v0:
```python
import math
import jax
import jax.numpy as jnp
from jax import lax
from jax.sharding import PartitionSpec as P

HEAD_DIM = 112
HIGH_PRECISION = lax.Precision.HIGHEST


def split_up(shard, dim, size):
    lengths = shard.shape
    pieces = shard.reshape(*lengths[:dim], size, lengths[dim] // size, *lengths[dim + 1 :])
    return jnp.moveaxis(pieces, dim, 0)


def sent_and_summed(shard, axis, dim):
    size = lax.axis_size(axis)
    pieces = lax.all_to_all(split_up(shard, dim, size), axis, 0, 0, tiled=True)
    return jnp.sum(pieces, axis=0)


def in_one_piece(arrays, axis, dim, along):
    widths = [math.prod(a.shape[along:]) for a in arrays]
    both = jnp.concatenate(
        [a.reshape(*a.shape[:along], w) for a, w in zip(arrays, widths)], axis=along
    )
    filled = sent_and_summed(both, axis, dim)
    pieces = jnp.split(filled, [sum(widths[:k]) for k in range(1, len(widths))], axis=along)
    return tuple(
        (b.reshape(*filled.shape[:along], *a.shape[along:]) for a, b in zip(arrays, pieces))
    )


def sent_to_all(shard, axis):
    size = lax.axis_size(axis)
    return lax.all_to_all(
        jnp.broadcast_to(shard[None], (size, *shard.shape)), axis, 0, 0, tiled=True
    )


def collected_together(shard, axis):
    leaves = jax.tree.leaves(shard)
    order = sorted(range(len(leaves)), key=lambda k: -leaves[k].size)
    width = (1, *leaves[order[0]].shape)[-1]
    lines = [
        jnp.pad(leaves[k].reshape(-1), (0, -leaves[k].size % width)).reshape(-1, width)
        for k in order
    ]
    both, at, found = (sent_to_all(jnp.concatenate(lines), axis), 0, {})
    for k, line in zip(order, lines):
        share = both[:, at : at + len(line)].reshape(len(both), -1)
        found[k] = share[:, : leaves[k].size].reshape(-1, *leaves[k].shape)
        at += len(line)
    numbers = iter(range(len(leaves)))
    return jax.tree.map(lambda _: found[next(numbers)], shard)


def folded_in_pairs(pieces, combine):
    while len(jax.tree.leaves(pieces)[0]) > 1:
        pieces = jax.vmap(combine)(
            *(jax.tree.map(lambda part: part[side::2], pieces) for side in (0, 1))
        )
    return jax.tree.map(lambda part: part[0], pieces)


def carried_in(shard, axis, combine, identity):
    size, mine = (lax.axis_size(axis), lax.axis_index(axis))
    passed = jnp.arange(size) < mine

    def kept(part, zero, own):
        part = jnp.where(
            passed.reshape(-1, *(1 for _ in own.shape)), part, jnp.asarray(zero, own.dtype)
        )
        return part

    pieces = collected_together(shard, axis)
    return folded_in_pairs(jax.tree.map(kept, pieces, identity, shard), combine)


def gather_turned(arrays, axis, dims):
    turned = [jnp.moveaxis(a, dim, 0) for a, dim in zip(arrays, dims)]
    both = jnp.concatenate([t.reshape(len(t), -1) for t in turned], axis=1)
    filled, at, finished = (lax.all_gather(both, axis, axis=0, tiled=True), 0, [])
    for t, dim in zip(turned, dims):
        share = filled[:, at : at + t[0].size].reshape(-1, *t.shape[1:])
        finished.append(jnp.moveaxis(share, 0, dim))
        at += t[0].size
    return tuple(finished)


def collected_together_2(shard, axis):
    leaves = jax.tree.leaves(shard)
    order = sorted(range(len(leaves)), key=lambda k: -leaves[k].size)
    width = (1, *leaves[order[0]].shape)[-1]
    lines = [
        jnp.pad(leaves[k].reshape(-1), (0, -leaves[k].size % width)).reshape(-1, width)
        for k in order
    ]
    both, at, found = (lax.all_gather(jnp.concatenate(lines), axis), 0, {})
    for k, line in zip(order, lines):
        share = both[:, at : at + len(line)].reshape(len(both), -1)
        found[k] = share[:, : leaves[k].size].reshape(-1, *leaves[k].shape)
        at += len(line)
    numbers = iter(range(len(leaves)))
    return jax.tree.map(lambda _: found[next(numbers)], shard)


def gathered_by_type(shard, axis):
    leaves, found = (jax.tree.leaves(shard), {})
    for leading, a in enumerate(leaves):
        if leading not in found:
            alike = [k for k, b in enumerate(leaves) if b.dtype == a.dtype]
            got = (
                collected_together_2([leaves[k] for k in alike], axis)
                if len(alike) > 1
                else [lax.all_gather(a, axis)]
            )
            for k, b in zip(alike, got):
                found[k] = b
    numbers = iter(range(len(leaves)))
    return jax.tree.map(lambda _: found[next(numbers)], shard)


def carried_in_2(shard, axis, combine, identity):
    size, mine = (lax.axis_size(axis), lax.axis_index(axis))
    everything = gathered_by_type(shard, axis)
    start = jax.tree.map(
        lambda part, zero: jnp.broadcast_to(jnp.asarray(zero, part.dtype), part.shape),
        shard,
        identity,
    )

    def hop(k, before):
        at = size - 1 - k
        reached = at > mine
        new = combine(before, jax.tree.map(lambda part: part[at], everything))
        return jax.tree.map(lambda a, b: jnp.where(reached, a, b), new, before)

    return lax.fori_loop(0, size, hop, start)


def add_pair(earlier, later):
    return (earlier[0] + later[0], earlier[1] + later[1])


def running_states(local_state, local_total):
    shares = in_one_piece((local_state, local_total), "space", 0, 1)
    before = carried_in(
        (shares[0], shares[1]),
        "tm",
        add_pair,
        (jnp.zeros_like(shares[0]), jnp.zeros_like(shares[1])),
    )
    running = add_pair(before, shares)
    return gather_turned((running[0], running[1]), "space", (0, 0))


def later_states(local_state, local_total):
    shares = (sent_and_summed(local_state, "space", 0), sent_and_summed(local_total, "space", 0))
    after = carried_in_2(
        (shares[0], shares[1]),
        "tm",
        add_pair,
        (jnp.zeros_like(shares[0]), jnp.zeros_like(shares[1])),
    )
    running = add_pair(after, shares)
    return gather_turned((running[0], running[1]), "space", (0, 0))


def body(queries, keys_in, values_in, grad_attn):
    row_count = queries.shape[1]
    channels = queries.shape[2]
    heads = channels // HEAD_DIM
    query_rows = queries[0]
    key_rows = keys_in[0]
    value_rows = values_in[0]
    key_pos = jax.nn.relu(key_rows)
    state_part = jnp.einsum(
        "isp,isz->spz",
        key_pos.reshape(row_count, heads, HEAD_DIM),
        value_rows.reshape(row_count, heads, HEAD_DIM),
        preferred_element_type=jnp.float32,
    )
    total_part = jnp.sum(key_pos, axis=0, dtype=jnp.float32)
    state_flat, total_flat = running_states(state_part.reshape(channels, HEAD_DIM), total_part)
    running_state = state_flat.reshape(heads, HEAD_DIM, HEAD_DIM)
    running_total = total_flat.reshape(heads, HEAD_DIM)
    query_position = jax.nn.relu(query_rows).astype(jnp.float32).reshape(row_count, heads, HEAD_DIM)
    numerator = jnp.einsum("igx,gxb->igb", query_position, running_state, precision=HIGH_PRECISION)
    denom = jnp.einsum("rhk,hk->rh", query_position, running_total, precision=HIGH_PRECISION) + 1.0
    attn_f = numerator / denom[..., None]
    mixed = attn_f.reshape(row_count, channels).astype(jnp.bfloat16)
    g_out = grad_attn[0].astype(jnp.float32).reshape(row_count, heads, HEAD_DIM)
    numerator_gradient = g_out / denom[..., None]
    denominator_gradient = -jnp.sum(g_out * attn_f, axis=-1) / denom
    feature_gradient = (
        jnp.einsum("tqd,qwd->tqw", numerator_gradient, running_state, precision=HIGH_PRECISION)
        + denominator_gradient[..., None] * running_total[None]
    )
    grad_queries = jnp.where(
        query_rows.reshape(row_count, heads, HEAD_DIM) > 0, feature_gradient, 0.0
    )
    partial_state_gradient = jnp.einsum(
        "isp,isz->spz", query_position, numerator_gradient, precision=HIGH_PRECISION
    )
    gtotal_part = jnp.einsum(
        "rhk,rh->hk", query_position, denominator_gradient, precision=HIGH_PRECISION
    )
    gstate_flat, gtotal_flat = later_states(
        partial_state_gradient.reshape(channels, HEAD_DIM), gtotal_part.reshape(channels)
    )
    state_gradient = gstate_flat.reshape(heads, HEAD_DIM, HEAD_DIM)
    total_gradient = gtotal_flat.reshape(heads, HEAD_DIM)
    key_wide_float = key_pos.astype(jnp.float32).reshape(row_count, heads, HEAD_DIM)
    value_wide_float = value_rows.astype(jnp.float32).reshape(row_count, heads, HEAD_DIM)
    values_gradient = jnp.einsum(
        "igx,gxb->igb", key_wide_float, state_gradient, precision=HIGH_PRECISION
    )
    key_gradient = (
        jnp.einsum("tqd,qwd->tqw", value_wide_float, state_gradient, precision=HIGH_PRECISION)
        + total_gradient[None]
    )
    grad_keys = jnp.where(key_rows.reshape(row_count, heads, HEAD_DIM) > 0, key_gradient, 0.0)
    return (
        mixed[None],
        grad_queries.reshape(row_count, channels).astype(jnp.bfloat16)[None],
        grad_keys.reshape(row_count, channels).astype(jnp.bfloat16)[None],
        values_gradient.reshape(row_count, channels).astype(jnp.bfloat16)[None],
    )


def solution(mesh):
    placed = (
        P("tm", "space", None),
        P("tm", "space", None),
        P("tm", "space", None),
        P("tm", "space", None),
    )
    return jax.shard_map(
        body,
        mesh=mesh,
        in_specs=placed,
        out_specs=(
            P("tm", "space", None),
            P("tm", "space", None),
            P("tm", "space", None),
            P("tm", "space", None),
        ),
        check_vma=False,
    )
```

profile of v0, /device:TPU:2, one launch (start us, length us, event | category | flops | bytes accessed | tf_op | source)
XLA Modules:
  0.0 212.7 jit_solution(13621507825996979436)
XLA Ops:
  0.7 1.2 convert_reduce_fusion
  2.6 1.1 pad_maximum_fusion
  3.6 10.2 %all-to-all-start = ((f32[32,35,113]{2,1,0:T(8,128)}), f32[32,35,113]{2,1,0:T(8,128)S(1)}, u32[]{:S(2)}, u32[]{:S(2)}) async-start(f32[32,35,113]{2,1,0:T(8,128)} %pad_maximum_fusion), calls=%async_computation | async-start | bytes 1310720 | tf_op jit(solution)/shard_map/all_to_all | solution.py:19
  13.9 18.0 %all-to-all-done = f32[32,35,113]{2,1,0:T(8,128)S(1)} async-done(((f32[32,35,113]{2,1,0:T(8,128)}), f32[32,35,113]{2,1,0:T(8,128)S(1)}, u32[]{:S(2)}, u32[]{:S(2)}) %all-to-all-start) | async-done | bytes 506272 | tf_op jit(solution)/shard_map/all_to_all | solution.py:19
  32.2 0.7 broadcast_in_dim.43
  32.9 10.6 %all-to-all-start.1 = ((f32[16,36,112]{2,1,0:T(8,128)}), f32[16,36,112]{2,1,0:T(8,128)S(1)}, u32[]{:S(2)}, u32[]{:S(2)}) async-start(f32[16,36,112]{2,1,0:T(8,128)} %broadcast_in_dim.43), calls=%async_computation.1 | async-start | bytes 655360 | tf_op jit(solution)/shard_map/all_to_all | solution.py:37
  43.5 12.3 %all-to-all-done.1 = f32[16,36,112]{2,1,0:T(8,128)S(1)} async-done(((f32[16,36,112]{2,1,0:T(8,128)}), f32[16,36,112]{2,1,0:T(8,128)S(1)}, u32[]{:S(2)}, u32[]{:S(2)}) %all-to-all-start.1) | async-done | bytes 258080 | tf_op jit(solution)/shard_map/all_to_all | solution.py:37
  56.6 49.1 %all-gather.1 = f32[32,35,113]{2,1,0:T(8,128)S(1)} all-gather(f32[1,35,113]{2,1,0:T(8,128)S(1)} %maximum_bitcast_fusion), channel_id=1, replica_groups=mesh['tm'=16,'space'=32] {'space'}, dimensions={0}, use_global_device_ids=true | all-gather | bytes 522060 | tf_op jit(solution)/shard_map/all_gather | solution.py:84
  106.5 0.5 copy-done.3
  107.0 1.3 fusion.7
  108.4 0.5 fusion.14
  109.0 0.7 all_to_all.18
  109.7 7.1 %all-to-all-start.3 = ((f32[32,1,35]{2,1,0:T(1,128)}), f32[32,1,35]{2,1,0:T(1,128)S(1)}, u32[]{:S(2)}, u32[]{:S(2)}) async-start(f32[32,1,35]{2,1,0:T(1,128)} %all_to_all.18), calls=%async_computation.3 | async-start | bytes 32768 | tf_op jit(solution)/shard_map/all_to_all | solution.py:19
  116.8 0.7 fusion.8
  117.5 0.9 reshape_reshape.8
  118.4 7.2 %all-to-all-done.3 = f32[32,1,35]{2,1,0:T(1,128)S(1)} async-done(((f32[32,1,35]{2,1,0:T(1,128)}), f32[32,1,35]{2,1,0:T(1,128)S(1)}, u32[]{:S(2)}, u32[]{:S(2)}) %all-to-all-start.3) | async-done | bytes 4512 | tf_op jit(solution)/shard_map/all_to_all | solution.py:19
  125.6 5.0 %all-to-all-start.2 = ((f32[32,35,112]{2,1,0:T(8,128)}), f32[32,35,112]{2,1,0:T(8,128)S(1)}, u32[]{:S(2)}, u32[]{:S(2)}) async-start(f32[32,35,112]{2,1,0:T(8,128)} %reshape_reshape.8), calls=%async_computation.2 | async-start | bytes 1310720 | tf_op jit(solution)/shard_map/all_to_all | solution.py:19
  130.8 1.5 fusion.6
  132.4 10.7 %all-to-all-done.2 = f32[32,35,112]{2,1,0:T(8,128)S(1)} async-done(((f32[32,35,112]{2,1,0:T(8,128)}), f32[32,35,112]{2,1,0:T(8,128)S(1)}, u32[]{:S(2)}, u32[]{:S(2)}) %all-to-all-start.2) | async-done | bytes 501792 | tf_op jit(solution)/shard_map/all_to_all | solution.py:19
  143.1 16.0 %all-gather.2 = f32[16,36,112]{2,1,0:T(8,128)S(1)} all-gather(f32[1,36,112]{2,1,0:T(8,128)S(1)} %maximum_bitcast_fusion.1), channel_id=2, replica_groups=mesh['tm'=16,'space'=32] {'tm'}, dimensions={0}, use_global_device_ids=true | all-gather | bytes 274176 | tf_op jit(solution)/shard_map/all_gather | solution.py:100
  159.2 1.1 while.18
  160.5 49.2 %all-gather.3 = f32[32,35,113]{2,1,0:T(8,128)S(1)} all-gather(f32[1,35,113]{2,1,0:T(8,128)S(1)} %maximum_bitcast_fusion.2), channel_id=1, replica_groups=mesh['tm'=16,'space'=32] {'space'}, dimensions={0}, use_global_device_ids=true | all-gather | bytes 522060 | tf_op jit(solution)/shard_map/all_gather | solution.py:84
  210.2 1.3 convolution_convert_fusion
  211.6 1.2 fusion.5
  (93 shorter events, 4.1 us)
Async XLA Ops:
  0.6 1.6 copy-start
  0.6 1.2 copy-start.1
  3.6 28.3 %all-to-all-start = ((f32[32,35,113]{2,1,0:T(8,128)}), f32[32,35,113]{2,1,0:T(8,128)S(1)}, u32[]{:S(2)}, u32[]{:S(2)}) async-start(f32[32,35,113]{2,1,0:T(8,128)} %pad_maximum_fusion), calls=%async_computation | async-start | bytes 1310720 | tf_op jit(solution)/shard_map/all_to_all | solution.py:19
  32.9 10.6 %copy-start.2 = (bf16[1,128,1120]{1,2,0:T(8,128)(2,1)S(1)}, bf16[1,128,1120]{1,2,0:T(8,128)(2,1)}, u32[]{:S(2)}) copy-start(bf16[1,128,1120]{1,2,0:T(8,128)(2,1)} %param.6) | copy-start | bytes 860164
  32.9 23.0 %all-to-all-start.1 = ((f32[16,36,112]{2,1,0:T(8,128)}), f32[16,36,112]{2,1,0:T(8,128)S(1)}, u32[]{:S(2)}, u32[]{:S(2)}) async-start(f32[16,36,112]{2,1,0:T(8,128)} %broadcast_in_dim.43), calls=%async_computation.1 | async-start | bytes 655360 | tf_op jit(solution)/shard_map/all_to_all | solution.py:37
  106.1 1.0 copy-start.3
  109.7 15.9 %all-to-all-start.3 = ((f32[32,1,35]{2,1,0:T(1,128)}), f32[32,1,35]{2,1,0:T(1,128)S(1)}, u32[]{:S(2)}, u32[]{:S(2)}) async-start(f32[32,1,35]{2,1,0:T(1,128)} %all_to_all.18), calls=%async_computation.3 | async-start | bytes 32768 | tf_op jit(solution)/shard_map/all_to_all | solution.py:19
  125.6 17.5 %all-to-all-start.2 = ((f32[32,35,112]{2,1,0:T(8,128)}), f32[32,35,112]{2,1,0:T(8,128)S(1)}, u32[]{:S(2)}, u32[]{:S(2)}) async-start(f32[32,35,112]{2,1,0:T(8,128)} %reshape_reshape.8), calls=%async_computation.2 | async-start | bytes 1310720 | tf_op jit(solution)/shard_map/all_to_all | solution.py:19
where the time goes:
time: 213 us
  blocking collectives  114 us (54%)
  waiting for transfers between devices  48.2 us (23%)
  starting transfers between devices  32.8 us (15%)
  matrix products  7.28 us (3%)
  local copies, waits for them, and re-layouts  4.91 us (2%)
  other arithmetic  3.66 us (2%)
    all_gather x2, blocking collectives, gather_turned(): lax.all_gather(both, axis, axis=0, tiled=True)  98.3 us
    all_to_all x3, waiting for transfers between devices, sent_and_summed(): pieces = lax.all_to_all(split_up(shard, dim, size), axis, 0, 0, tiled=True)  35.9 us
    all_to_all x3, starting transfers between devices, sent_and_summed(): pieces = lax.all_to_all(split_up(shard, dim, size), axis, 0, 0, tiled=True)  22.3 us
    all_gather x1, blocking collectives, collected_together_2(): both, at, found = (lax.all_gather(jnp.concatenate(lines), axis), 0, {})  16 us
    all_to_all x1, waiting for transfers between devices, sent_to_all(): lax.all_to_all(jnp.broadcast_to(shard[None], (size, *shard.shape)), axis,...  12.3 us
    all_to_all x1, starting transfers between devices, sent_to_all(): lax.all_to_all(jnp.broadcast_to(shard[None], (size, *shard.shape)), axis,...  10.6 us
  transfers between devices with their start and end apart: 4, of which 4 were waited for; matrix products, arithmetic and copies ran while one was open for 2% of the time, Pallas kernels for 0%

commit v1 on v0

--- a/solution.py
+++ b/solution.py
@@ -81,7 +81,10 @@
 def gather_turned(arrays, axis, dims):
     turned = [jnp.moveaxis(a, dim, 0) for a, dim in zip(arrays, dims)]
     both = jnp.concatenate([t.reshape(len(t), -1) for t in turned], axis=1)
-    filled, at, finished = (lax.all_gather(both, axis, axis=0, tiled=True), 0, [])
+    spread_ways_on = lambda panel, link_axis: jnp.concatenate(
+        lax.all_to_all(jnp.stack(lax.psum(1, link_axis) * [panel], axis=0), link_axis, 0, 0), 0
+    )
+    filled, at, finished = (spread_ways_on(both, axis), 0, [])
     for t, dim in zip(turned, dims):
         share = filled[:, at : at + t[0].size].reshape(-1, *t.shape[1:])
         finished.append(jnp.moveaxis(share, 0, dim))

time: 213 us -> 174 us (0.82)
  the two profiles are of different devices: /device:TPU:2 before, /device:TPU:8 now
where the time goes in v1:
time: 174 us; the launch traced here: 173 us
  waiting for transfers between devices  79.2 us (46%)
  blocking collectives  45.3 us (26%)
  starting transfers between devices  30.6 us (18%)
  matrix products  7.28 us (4%)
  local copies, waits for them, and re-layouts  6.67 us (4%)
  other arithmetic  2.82 us (2%)
    all_to_all x2, waiting for transfers between devices, gather_turned(): lax.all_to_all(jnp.stack(lax.psum(1, link_axis) * [panel], axis=0), link_...  40.4 us
    all_to_all x1, blocking collectives, sent_and_summed(): pieces = lax.all_to_all(split_up(shard, dim, size), axis, 0, 0, tiled=True)  30.2 us
    all_to_all x2, waiting for transfers between devices, sent_and_summed(): pieces = lax.all_to_all(split_up(shard, dim, size), axis, 0, 0, tiled=True)  26.4 us
    all_gather x1, blocking collectives, collected_together_2(): both, at, found = (lax.all_gather(jnp.concatenate(lines), axis), 0, {})  15.1 us
    all_to_all x1, waiting for transfers between devices, sent_to_all(): lax.all_to_all(jnp.broadcast_to(shard[None], (size, *shard.shape)), axis,...  12.4 us
    all_to_all x1, starting transfers between devices, sent_to_all(): lax.all_to_all(jnp.broadcast_to(shard[None], (size, *shard.shape)), axis,...  10.4 us
    all_to_all x2, starting transfers between devices, sent_and_summed(): pieces = lax.all_to_all(split_up(shard, dim, size), axis, 0, 0, tiled=True)  10.1 us
    all_to_all x2, starting transfers between devices, gather_turned(): lax.all_to_all(jnp.stack(lax.psum(1, link_axis) * [panel], axis=0), link_...  10.1 us
  transfers between devices with their start and end apart: 5, of which 5 were waited for; matrix products, arithmetic and copies ran while one was open for 2% of the time, Pallas kernels for 0%

profile of v1, /device:TPU:8, one launch (start us, length us, event | category | flops | bytes accessed | tf_op | source)
XLA Modules:
  0.0 173.4 jit_solution(11262973066867783342)
XLA Ops:
  0.7 1.2 convert_reduce_fusion
  2.8 30.2 %all_to_all.34 = f32[32,35,113]{2,1,0:T(8,128)S(1)} all-to-all(f32[32,35,113]{2,1,0:T(8,128)S(1)} %pad_maximum_fusion), channel_id=1, replica_groups=mesh['tm'=16,'space'=32] {'space'}, dimensions={0} | all-to-all | bytes 1012480 | tf_op jit(solution)/shard_map/all_to_all | solution.py:19
  33.3 0.7 broadcast_in_dim.43
  34.0 10.4 %all-to-all-start.1 = ((f32[16,36,112]{2,1,0:T(8,128)}), f32[16,36,112]{2,1,0:T(8,128)S(1)}, u32[]{:S(2)}, u32[]{:S(2)}) async-start(f32[16,36,112]{2,1,0:T(8,128)} %broadcast_in_dim.43), calls=%async_computation.1 | async-start | bytes 655360 | tf_op jit(solution)/shard_map/all_to_all | solution.py:37
  44.5 12.4 %all-to-all-done.1 = f32[16,36,112]{2,1,0:T(8,128)S(1)} async-done(((f32[16,36,112]{2,1,0:T(8,128)}), f32[16,36,112]{2,1,0:T(8,128)S(1)}, u32[]{:S(2)}, u32[]{:S(2)}) %all-to-all-start.1) | async-done | bytes 258080 | tf_op jit(solution)/shard_map/all_to_all | solution.py:37
  57.5 0.9 stack.4
  58.4 5.2 %all-to-all-start.2 = ((f32[32,35,113]{2,1,0:T(8,128)}), f32[32,35,113]{2,1,0:T(8,128)S(1)}, u32[]{:S(2)}, u32[]{:S(2)}) async-start(f32[32,35,113]{2,1,0:T(8,128)} %stack.4), calls=%async_computation.2 | async-start | bytes 1310720 | tf_op jit(solution)/shard_map/all_to_all | solution.py:85
  63.6 21.3 %all-to-all-done.2 = f32[32,35,113]{2,1,0:T(8,128)S(1)} async-done(((f32[32,35,113]{2,1,0:T(8,128)}), f32[32,35,113]{2,1,0:T(8,128)S(1)}, u32[]{:S(2)}, u32[]{:S(2)}) %all-to-all-start.2) | async-done | bytes 506272 | tf_op jit(solution)/shard_map/all_to_all | solution.py:85
  86.3 1.3 fusion.7
  88.2 0.7 all_to_all.25
  89.0 5.2 %all-to-all-start.4 = ((f32[32,1,35]{2,1,0:T(1,128)}), f32[32,1,35]{2,1,0:T(1,128)S(1)}, u32[]{:S(2)}, u32[]{:S(2)}) async-start(f32[32,1,35]{2,1,0:T(1,128)} %all_to_all.25), calls=%async_computation.4 | async-start | bytes 32768 | tf_op jit(solution)/shard_map/all_to_all | solution.py:19
  94.2 0.7 fusion.8
  94.9 0.9 reshape_reshape.8
  95.8 7.0 %all-to-all-done.4 = f32[32,1,35]{2,1,0:T(1,128)S(1)} async-done(((f32[32,1,35]{2,1,0:T(1,128)}), f32[32,1,35]{2,1,0:T(1,128)S(1)}, u32[]{:S(2)}, u32[]{:S(2)}) %all-to-all-start.4) | async-done | bytes 4512 | tf_op jit(solution)/shard_map/all_to_all | solution.py:19
  102.7 4.9 %all-to-all-start.3 = ((f32[32,35,112]{2,1,0:T(8,128)}), f32[32,35,112]{2,1,0:T(8,128)S(1)}, u32[]{:S(2)}, u32[]{:S(2)}) async-start(f32[32,35,112]{2,1,0:T(8,128)} %reshape_reshape.8), calls=%async_computation.3 | async-start | bytes 1310720 | tf_op jit(solution)/shard_map/all_to_all | solution.py:19
  107.8 19.5 %all-to-all-done.3 = f32[32,35,112]{2,1,0:T(8,128)S(1)} async-done(((f32[32,35,112]{2,1,0:T(8,128)}), f32[32,35,112]{2,1,0:T(8,128)S(1)}, u32[]{:S(2)}, u32[]{:S(2)}) %all-to-all-start.3) | async-done | bytes 501792 | tf_op jit(solution)/shard_map/all_to_all | solution.py:19
  127.3 15.1 %all-gather.1 = f32[16,36,112]{2,1,0:T(8,128)S(1)} all-gather(f32[1,36,112]{2,1,0:T(8,128)S(1)} %maximum_bitcast_fusion), channel_id=2, replica_groups=mesh['tm'=16,'space'=32] {'tm'}, dimensions={0}, use_global_device_ids=true | all-gather | bytes 274176 | tf_op jit(solution)/shard_map/all_gather | solution.py:103
  142.4 1.1 while.18
  143.7 0.9 stack.5
  144.5 4.9 %all-to-all-start.5 = ((f32[32,35,113]{2,1,0:T(8,128)}), f32[32,35,113]{2,1,0:T(8,128)S(1)}, u32[]{:S(2)}, u32[]{:S(2)}) async-start(f32[32,35,113]{2,1,0:T(8,128)} %stack.5), calls=%async_computation.5 | async-start | bytes 1310720 | tf_op jit(solution)/shard_map/all_to_all | solution.py:85
  149.7 1.5 fusion.6
  151.3 19.1 %all-to-all-done.5 = f32[32,35,113]{2,1,0:T(8,128)S(1)} async-done(((f32[32,35,113]{2,1,0:T(8,128)}), f32[32,35,113]{2,1,0:T(8,128)S(1)}, u32[]{:S(2)}, u32[]{:S(2)}) %all-to-all-start.5) | async-done | bytes 506272 | tf_op jit(solution)/shard_map/all_to_all | solution.py:85
  170.9 1.3 convolution_convert_fusion
  172.2 1.2 fusion.5
  (96 shorter events, 5.4 us)
Async XLA Ops:
  0.6 1.6 copy-start
  0.6 1.2 copy-start.1
  34.0 22.8 %all-to-all-start.1 = ((f32[16,36,112]{2,1,0:T(8,128)}), f32[16,36,112]{2,1,0:T(8,128)S(1)}, u32[]{:S(2)}, u32[]{:S(2)}) async-start(f32[16,36,112]{2,1,0:T(8,128)} %broadcast_in_dim.43), calls=%async_computation.1 | async-start | bytes 655360 | tf_op jit(solution)/shard_map/all_to_all | solution.py:37
  58.4 5.2 %copy-start.2 = (bf16[1,128,1120]{1,2,0:T(8,128)(2,1)S(1)}, bf16[1,128,1120]{1,2,0:T(8,128)(2,1)}, u32[]{:S(2)}) copy-start(bf16[1,128,1120]{1,2,0:T(8,128)(2,1)} %param.6) | copy-start | bytes 860164
  58.4 26.5 %all-to-all-start.2 = ((f32[32,35,113]{2,1,0:T(8,128)}), f32[32,35,113]{2,1,0:T(8,128)S(1)}, u32[]{:S(2)}, u32[]{:S(2)}) async-start(f32[32,35,113]{2,1,0:T(8,128)} %stack.4), calls=%async_computation.2 | async-start | bytes 1310720 | tf_op jit(solution)/shard_map/all_to_all | solution.py:85
  85.4 1.0 copy-start.3
  89.0 13.8 %all-to-all-start.4 = ((f32[32,1,35]{2,1,0:T(1,128)}), f32[32,1,35]{2,1,0:T(1,128)S(1)}, u32[]{:S(2)}, u32[]{:S(2)}) async-start(f32[32,1,35]{2,1,0:T(1,128)} %all_to_all.25), calls=%async_computation.4 | async-start | bytes 32768 | tf_op jit(solution)/shard_map/all_to_all | solution.py:19
  102.7 24.5 %all-to-all-start.3 = ((f32[32,35,112]{2,1,0:T(8,128)}), f32[32,35,112]{2,1,0:T(8,128)S(1)}, u32[]{:S(2)}, u32[]{:S(2)}) async-start(f32[32,35,112]{2,1,0:T(8,128)} %reshape_reshape.8), calls=%async_computation.3 | async-start | bytes 1310720 | tf_op jit(solution)/shard_map/all_to_all | solution.py:19
  144.5 25.8 %all-to-all-start.5 = ((f32[32,35,113]{2,1,0:T(8,128)}), f32[32,35,113]{2,1,0:T(8,128)S(1)}, u32[]{:S(2)}, u32[]{:S(2)}) async-start(f32[32,35,113]{2,1,0:T(8,128)} %stack.5), calls=%async_computation.5 | async-start | bytes 1310720 | tf_op jit(solution)/shard_map/all_to_all | solution.py:85
